TPU v7x, 32 devices: a whole 2x2x4 slice. The times are simulated.
32 devices in a mesh: dp: 2 (over y), cls: 16 (over z, x, core).
Axes of the slice: x: 2, y: 2, z: 4, core: 2. Of those that a mesh axis runs over, the one named last changes fastest.
Arguments:
- embeddings: bfloat16 [1152, 4096], P('dp'), may hold values from -128 to 128
- fold_ids: int32 [1152], P('dp'), may hold values from 0 to 4
- labels: int32 [1152], P('dp'), may hold values from 0 to 1023
- weights: bfloat16 [4096, 5120], P('dp', 'cls'), may hold values from -4 to 4
- direction: bfloat16 [4096, 5120], P('dp', 'cls'), may hold values from -0.09375 to 0.09375
Outputs:
- gradient: float32 [4096, 5120], P('dp', 'cls')
- hess_vec: float32 [4096, 5120], P('dp', 'cls')
All inputs are finite; a program needn't handle non-finite values.
Results may differ from a plain program's by a relative error of at most 0.0055.
Values may be sent and summed in bfloat16 or wider, within the bound.
A program may use at most 64 MiB of HBM per device.

v0:
```python
import jax
import jax.numpy as jnp
from jax import lax
from jax.sharding import PartitionSpec as P

D = 4096
FOLDS = 5


def local(embeddings, fold_ids, labels, weights, direction):
    row_count = embeddings.shape[0]
    columns = weights.shape[1]
    per_class = columns // FOLDS
    logits = jnp.dot(
        embeddings,
        lax.all_gather(weights, "dp", axis=0, tiled=True),
        preferred_element_type=jnp.float32,
    )
    tangent = jnp.dot(
        embeddings,
        lax.all_gather(direction, "dp", axis=0, tiled=True),
        preferred_element_type=jnp.float32,
    )
    logits = logits.reshape(row_count, per_class, FOLDS)
    tangent = tangent.reshape(row_count, per_class, FOLDS)
    local_high = jnp.max(logits, axis=1)
    highest = lax.pmax(local_high, "cls")
    scaled = jnp.exp(logits - highest[:, None, :])
    summed, moment = lax.psum((jnp.sum(scaled, axis=1), jnp.sum(scaled * tangent, axis=1)), "cls")
    probability = scaled / summed[:, None, :]
    mean_tangent = moment / summed
    class_ids = lax.axis_index("cls") * per_class + jnp.arange(per_class, dtype=jnp.int32)
    onehot = (labels[:, None] == class_ids[None, :]).astype(jnp.float32)[:, :, None]
    training = (fold_ids[:, None] != jnp.arange(FOLDS, dtype=jnp.int32)[None, :]).astype(
        jnp.float32
    )[:, None, :]
    residual_rows = (
        (training * (probability - onehot)).reshape(row_count, columns).astype(jnp.bfloat16)
    )
    curvature = (
        (training * probability * (tangent - mean_tangent[:, None, :]))
        .reshape(row_count, columns)
        .astype(jnp.bfloat16)
    )
    contract = (((0,), (0,)), ((), ()))
    share = D // lax.axis_size("dp")
    full_grad, full_hvp = lax.psum(
        (
            lax.dot_general(
                embeddings, residual_rows, contract, preferred_element_type=jnp.float32
            ),
            lax.dot_general(embeddings, curvature, contract, preferred_element_type=jnp.float32),
        ),
        "dp",
    )
    offset = lax.axis_index("dp") * share
    gradient = lax.dynamic_slice_in_dim(full_grad, offset, share, 0)
    hess_vec = lax.dynamic_slice_in_dim(full_hvp, offset, share, 0)
    return (gradient, hess_vec)


def solution(mesh):
    placed = (P("dp", None), P("dp"), P("dp"), P("dp", "cls"), P("dp", "cls"))
    return jax.shard_map(
        local,
        mesh=mesh,
        in_specs=placed,
        out_specs=(P("dp", "cls"), P("dp", "cls")),
        check_vma=False,
    )
```

profile of v0, /device:TPU:0, one launch (start us, length us, event | category | flops | bytes accessed | tf_op | source)
XLA Modules:
  0.0 459.4 jit_solution(18000110894748950936)
XLA Ops:
  7.2 0.0 copy-start.4
  7.2 0.0 all-gather.3.cloned.1.call-start
  7.2 0.7 all-gather.3.cloned.1.call-update
  7.9 0.0 copy-start.3
  7.9 0.0 all-gather.5.cloned.1.call-start
  8.0 0.7 all-gather.5.cloned.1.call-update
  8.7 0.0 all-reduce.4.cloned.1.call-start
  8.7 0.0 copy-done.4
  8.7 0.1 compare_convert_fusion
  8.8 0.1 sub.40
  8.9 1.0 sub.41
  10.0 0.0 copy-done.3
  10.0 0.1 mul.31
  10.1 0.1 mul.32
  10.2 41.1 %all-gather.3.cloned.1.call-done = bf16[4096,320]{0,1:T(8,128)(2,1)} async-done(((bf16[2048,320]{0,1:T(8,128)(2,1)}), bf16[4096,320]{0,1:T(8,128)(2,1)}) %all-gather.3.cloned.1.call-update) | async-done | bytes 2621456 | tf_op jit(solution)/shard_map/all_gather | solution.py:16
  51.3 5.4 %fusion.2 = f32[576,320]{0,1:T(8,128)S(1)} fusion(bf16[576,4096]{1,0:T(8,128)(2,1)} %param.5, bf16[4096,320]{0,1:T(8,128)(2,1)} %all-gather.3.cloned.1.call-done), kind=kOutput, calls=%fused_computation.14 | convolution fusion | flops 1509949440 | bytes 8077312 | tf_op jit(solution)/shard_map/dot_general | solution.py:14
  56.7 0.1 reshape.74
  56.9 0.1 reduce_max.9
  57.0 61.2 %pmax.7 = f32[576,5]{0,1:T(8,128)S(1)} all-reduce(f32[576,5]{0,1:T(8,128)S(1)} %reduce_max.9), channel_id=1, replica_groups=mesh['dp'=2,'cls'=16] {'cls'}, use_global_device_ids=true, to_apply=%region_1.0 | all-reduce | flops 2880 | bytes 23040 | tf_op jit(solution)/shard_map/pmax | solution.py:27
  118.2 1.1 sub.36
  119.3 2.4 sub.37
  121.7 0.0 all-gather.5.cloned.1.call-done
  121.7 6.3 %fusion.3 = f32[576,320]{0,1:T(8,128)} fusion(bf16[576,4096]{1,0:T(8,128)(2,1)} %param.5, bf16[4096,320]{0,1:T(8,128)(2,1)} %all-gather.5.cloned.1.call-done), kind=kOutput, calls=%fused_computation.15 | convolution fusion | flops 1509949440 | bytes 8077312 | tf_op jit(solution)/shard_map/dot_general | solution.py:19
  128.0 2.3 reshape.75
  130.3 1.7 multiply_reduce_fusion
  132.0 57.7 %all-reduce = (f32[576,5]{0,1:T(8,128)S(1)}, f32[576,5]{0,1:T(8,128)S(1)}) all-reduce(f32[576,5]{0,1:T(8,128)S(1)} %get-tuple-element.3, f32[576,5]{0,1:T(8,128)S(1)} %get-tuple-element.2), channel_id=1, replica_groups=mesh['dp'=2,'cls'=16] {'cls'}, use_global_device_ids=true, to_apply=%region_3.0 | all-reduce | flops 5760 | bytes 46080 | tf_op jit(solution)/shard_map/psum | solution.py:29
  189.7 0.1 div.15
  189.8 1.1 div.16
  190.9 1.1 sub.43
  192.0 0.0 slice-start
  192.0 2.5 sub.44
  194.5 0.0 slice-start.1
  194.5 0.0 copy-start
  194.5 0.0 copy-start.1
  194.5 0.0 copy-start.2
  194.5 8.0 %convolution_bitcast_fusion = f32[4096,320]{0,1:T(8,128)} fusion(bf16[576,4096]{1,0:T(8,128)(2,1)} %param.5, f32[576,320]{0,1:T(8,128)} %fusion.3, f32[576,320]{0,1:T(8,128)} %sub.44, f32[576,320]{0,1:T(8,128)S(1)} %mul.32, f32[576,320]{0,1:T(8,128)} %div.16, f32[576,320]{0,1:T(8,128)S(1)} %fusion.2, f32[576,320]{0,1:T(8,128)} %sub.37), kind=kOutput, calls=%fused_computation | convolution fusion | flops 1511055360 | bytes 14385152 | tf_op jit(solution)/shard_map/dot_general | solution.py:52
  202.5 0.0 slice-done
  202.5 0.0 slice-done.1
  202.6 0.0 copy-done
  202.6 0.0 copy-done.1
  202.6 0.0 copy-done.2
  202.6 4.5 convolution_bitcast_fusion.1
  207.1 0.0 all-reduce.4.cloned.1.call-update
  207.1 240.2 %all-reduce.4.cloned.1.call-done = (f32[4096,320]{0,1:T(8,128)}, f32[4096,320]{0,1:T(8,128)}) async-done(((f32[4096,320]{0,1:T(8,128)}, f32[4096,320]{0,1:T(8,128)}), (f32[4096,320]{0,1:T(8,128)}, f32[4096,320]{0,1:T(8,128)})) %all-reduce.4.cloned.1.call-update) | async-done | bytes 10485776 | tf_op jit(solution)/shard_map/psum | solution.py:47
  447.3 5.5 %constant_dynamic-slice_fusion = (f32[2048,320]{0,1:T(8,128)}, f32[2048,320]{0,1:T(8,128)}) fusion(f32[4096,320]{0,1:T(8,128)} %get-tuple-element.7, s32[]{:T(128)S(6)} %select_n.4, f32[4096,320]{0,1:T(8,128)} %get-tuple-element.6), kind=kLoop, calls=%fused_computation.11 | loop fusion | bytes 10485764 | tf_op jit(solution)/shard_map/dynamic_slice | solution.py:58
  (4 shorter events, 0.0 us)
Async XLA Ops:
  7.2 1.6 copy-start.4
  7.2 44.1 %all-gather.3.cloned.1.call-start = ((), (), s32[]{:S(2)}) async-start(), calls=%async_computation | async-start | bytes 3932160 | tf_op jit(solution)/shard_map/all_gather | solution.py:16
  7.9 2.1 copy-start.3
  7.9 113.8 %all-gather.5.cloned.1.call-start = ((), (), s32[]{:S(2)}) async-start(), calls=%async_computation.1 | async-start | bytes 3932160 | tf_op jit(solution)/shard_map/all_gather | solution.py:21
  8.7 438.6 %all-reduce.4.cloned.1.call-start = ((), (), s32[]{:S(2)}) async-start(), calls=%async_computation.2 | async-start | bytes 20971520 | tf_op jit(solution)/shard_map/psum | solution.py:47
  192.0 10.5 %slice-start = ((s8[4718592]{0:T(1024)(128)(4,1)}), s8[524288]{0:T(1024)(128)(4,1)S(1)}, s32[]{:S(2)}) async-start(s8[4718592]{0:T(1024)(128)(4,1)} %bitcast.24), calls=%async_computation.3 | async-start | bytes 1048576
  194.5 8.0 %slice-start.1 = ((s8[4718592]{0:T(1024)(128)(4,1)}), s8[4194304]{0:T(1024)(128)(4,1)S(1)}, s32[]{:S(2)}) async-start(s8[4718592]{0:T(1024)(128)(4,1)} %bitcast.24), calls=%async_computation.4 | async-start | bytes 8388608
  194.5 8.0 %copy-start = (f32[576,320]{0,1:T(8,128)S(1)}, f32[576,320]{0,1:T(8,128)}, u32[]{:S(2)}) copy-start(f32[576,320]{0,1:T(8,128)} %sub.37) | copy-start | bytes 2211844
  194.5 8.1 %copy-start.1 = (f32[576,320]{0,1:T(8,128)S(1)}, f32[576,320]{0,1:T(8,128)}, u32[]{:S(2)}) copy-start(f32[576,320]{0,1:T(8,128)} %div.16) | copy-start | bytes 2211844
  194.5 8.1 %copy-start.2 = (f32[576,320]{0,1:T(8,128)S(1)}, f32[576,320]{0,1:T(8,128)}, u32[]{:S(2)}) copy-start(f32[576,320]{0,1:T(8,128)} %sub.41) | copy-start | bytes 2211844
Sparse Core Ops, SparseCore 0:
  9.6 41.7 all-gather.2
  52.9 39.0 all-gather.4
  207.2 240.0 all-reduce.3
where the time goes:
time: 460 us; the launch traced here: 459 us
  waiting for transfers between devices  283 us (62%)
  blocking collectives  119 us (26%)
  matrix products  24.2 us (5%)
  local copies, waits for them, and re-layouts  17.6 us (4%)
  between operations  13.9 us (3%)
    psum x1, waiting for transfers between devices, local(): lax.psum((lax.dot_general(embeddings, residual_rows, contract, preferred_...  240 us
    pmax x1, blocking collectives, local(): highest = lax.pmax(local_high, 'cls')  61.2 us
    psum x1, blocking collectives, local(): lax.psum((jnp.sum(scaled, axis=1), jnp.sum(scaled * tangent, axis=1)), 'c...  57.7 us
    all_gather x1, waiting for transfers between devices, local(): lax.all_gather(weights, 'dp', axis=0, tiled=True)  41.1 us
  transfers between devices with their start and end apart: 3, of which 2 were waited for; matrix products, arithmetic and copies ran while one was open for 2% of the time, Pallas kernels for 0%

commit v1 on v0

--- a/solution.py
+++ b/solution.py
@@ -1,6 +1,10 @@
+import functools
+
 import jax
 import jax.numpy as jnp
 from jax import lax
+from jax.experimental import pallas as pl
+from jax.experimental.pallas import tpu as pltpu
 from jax.sharding import PartitionSpec as P
 
 D = 4096
@@ -59,10 +63,326 @@
     return (gradient, hess_vec)
 
 
+MESH = pl.DeviceIdType.MESH
+LANES = 128
+SLOTS = FOLDS - 1
+NT = (((1,), (1,)), ((), ()))
+
+
+def pack(nat, base, per, fold):
+    blocks = [nat[pl.ds(base + f, per, stride=FOLDS), :] for f in range(FOLDS)]
+    return [jnp.where(fold > s, blocks[s], blocks[s + 1]) for s in range(SLOTS)]
+
+
+def unpack(slots, nat, base, per, fold):
+    for f in range(FOLDS):
+        if f == 0:
+            block = slots[0]
+        elif f == FOLDS - 1:
+            block = slots[SLOTS - 1]
+        else:
+            block = jnp.where(fold > f, slots[f], slots[f - 1])
+        nat[pl.ds(base + f, per, stride=FOLDS), :] = jnp.where(fold == f, 0.0, block)
+
+
+def merge(parts):
+    high = functools.reduce(jnp.maximum, [p[0] for p in parts])
+    total, moment = 0.0, 0.0
+    for m, s, t in parts:
+        w = jnp.exp(m - high)
+        total = total + s * w
+        moment = moment + t * w
+    return high, total, moment
+
+
+def split_stats(tile):
+    return tile[0:4], tile[4:8], tile[8:12]
+
+
+def exchange(
+    e, wt, dt, aux, rown, rpeer, epout,
+    wd, em, ep, auxp, nat, xsend, xrecv, xtot, so1, si1, so2, si2, rsend, rrecv,
+    lsem, asem, ys, yr, xs, xr, c1s, c1r, c2s, c2r, ps, pr, s1s, s1r, s2s, s2r, rs, rr,
+):
+    rows, share = em.shape
+    cols = wt.shape[0]
+    per = cols // FOLDS
+    packed = SLOTS * per
+    quarter = share // 4
+    chunks = xsend.shape[0]
+    starts = [min(LANES * k, rows - LANES) for k in range(chunks)]
+    pieces = [(LANES * k, min(LANES, rows - LANES * k)) for k in range(chunks)]
+
+    d = lax.axis_index("dp")
+    cls = lax.axis_index("cls")
+    c = cls % 2
+    x = (cls // 2) % 2
+    z = cls // 4
+    q = 2 * x + c
+    other = 1 - d
+    core = cls + 1 - 2 * c
+    xn = cls + 2 - 4 * x
+    group = [core, xn, cls + 3 - 2 * c - 4 * x]
+    zs = [z + 1 - 2 * (z % 2), z + 2 - 4 * (z // 2), 3 - z]
+    zgroup = [4 * zz + q for zz in zs]
+    peer = (other, cls)
+
+    loads = [
+        pltpu.make_async_copy(wt, wd.at[pl.ds(0, cols)], lsem.at[0]),
+        pltpu.make_async_copy(dt, wd.at[pl.ds(cols, cols)], lsem.at[1]),
+        pltpu.make_async_copy(
+            e.at[:, pl.ds(pl.multiple_of(d * share, share), share)], em, lsem.at[2]
+        ),
+    ]
+    for load in loads:
+        load.start()
+
+    barrier = pltpu.get_barrier_semaphore()
+    partners = [peer] + [(d, g) for g in group] + [(d, g) for g in zgroup]
+    for partner in partners:
+        pl.semaphore_signal(barrier, inc=1, device_id=partner, device_id_type=MESH)
+    pl.semaphore_wait(barrier, len(partners))
+
+    def remote(src, dst, send, recv, to):
+        return pltpu.make_async_remote_copy(
+            src_ref=src, dst_ref=dst, send_sem=send, recv_sem=recv,
+            device_id=to, device_id_type=MESH,
+        )
+
+    qa = pl.ds(pl.multiple_of(q * quarter, quarter), quarter)
+    qb = pl.ds(pl.multiple_of((q + 2 - 4 * x) * quarter, quarter), quarter)
+    qs = pl.ds(pl.multiple_of(other * share + q * quarter, quarter), quarter)
+
+    acopy = remote(aux, auxp, asem.at[0], asem.at[1], peer)
+    ycopy, xcopy, c1copy, c2copy = [], [], [], []
+    for t, (at, size) in enumerate(pieces):
+        r = pl.ds(at, size)
+        ycopy.append(remote(e.at[r, qs], ep.at[r, qa], ys.at[t], yr.at[t], peer))
+        xcopy.append(remote(ep.at[r, qa], ep.at[r, qa], xs.at[t], xr.at[t], (d, xn)))
+        c1copy.append(remote(ep.at[r, qa], ep.at[r, qa], c1s.at[t], c1r.at[t], (d, core)))
+        c2copy.append(remote(ep.at[r, qb], ep.at[r, qb], c2s.at[t], c2r.at[t], (d, core)))
+    pcopy = [remote(xsend.at[k], xrecv.at[k], ps.at[k], pr.at[k], peer) for k in range(chunks)]
+    rcopy = [remote(rsend.at[k], rrecv.at[k], rs.at[k], rr.at[k], peer) for k in range(chunks)]
+    s1copy = [
+        [remote(so1.at[k], si1.at[k, j], s1s.at[k, j], s1r.at[k, j], (d, g)) for j, g in enumerate(group)]
+        for k in range(chunks)
+    ]
+    s2copy = [
+        [remote(so2.at[k], si2.at[k, j], s2s.at[k, j], s2r.at[k, j], (d, g)) for j, g in enumerate(zgroup)]
+        for k in range(chunks)
+    ]
+
+    acopy.start()
+    for copy in ycopy:
+        copy.start()
+    for load in loads:
+        load.wait()
+
+    def partial_slots(emb, k, fold, out):
+        nat[...] = lax.dot_general(
+            wd[...], emb[pl.ds(starts[k], LANES), :], NT, preferred_element_type=jnp.float32
+        )
+        for half in range(2):
+            for s, block in enumerate(pack(nat, half * cols, per, fold)):
+                out[k, pl.ds(half * packed + s * per, per), :] = block
+
+    def stage_a(t):
+        ycopy[t].wait_recv()
+        xcopy[t].start()
+        c1copy[t].start()
+
+    def stage_b(t):
+        xcopy[t].wait_recv()
+        c2copy[t].start()
+
+    def stage_o(k):
+        partial_slots(em, k, aux[k, 0:1, :], xtot)
+
+    def stage_c(k):
+        if k == 0:
+            acopy.wait_recv()
+        c1copy[k].wait_recv()
+        c2copy[k].wait_recv()
+        partial_slots(ep, k, auxp[k, 0:1, :], xsend)
+        pcopy[k].start()
+
+    def slot(ref, k, half, s):
+        return ref[k, pl.ds(half * packed + s * per, per), :]
+
+    def stage_d(k):
+        pcopy[k].wait_recv()
+        xtot[k] = xtot[k] + xrecv[k]
+        for s in range(SLOTS):
+            logit = slot(xtot, k, 0, s)
+            high = jnp.max(logit, axis=0, keepdims=True)
+            scaled = jnp.exp(logit - high)
+            so1[k, s : s + 1, :] = high
+            so1[k, 4 + s : 5 + s, :] = jnp.sum(scaled, axis=0, keepdims=True)
+            so1[k, 8 + s : 9 + s, :] = jnp.sum(scaled * slot(xtot, k, 1, s), axis=0, keepdims=True)
+        so1[k, 12:16, :] = jnp.zeros((4, LANES), jnp.float32)
+        for copy in s1copy[k]:
+            copy.start()
+
+    def merged(own, incoming, k):
+        return merge([split_stats(own[k])] + [split_stats(incoming[k, j]) for j in range(3)])
+
+    def stage_e(k):
+        for copy in s1copy[k]:
+            copy.wait_recv()
+        high, total, moment = merged(so1, si1, k)
+        so2[k, 0:4, :] = high
+        so2[k, 4:8, :] = total
+        so2[k, 8:12, :] = moment
+        so2[k, 12:16, :] = jnp.zeros((4, LANES), jnp.float32)
+        for copy in s2copy[k]:
+            copy.start()
+
+    def place(out, k):
+        keep = starts[k] - LANES * k
+        if keep:
+            out[:, pl.ds(LANES * k, LANES + keep)] = nat[:, -keep:].astype(jnp.bfloat16)
+        else:
+            out[:, pl.ds(LANES * k, LANES)] = nat[...].astype(jnp.bfloat16)
+
+    def stage_f(k):
+        for copy in s2copy[k]:
+            copy.wait_recv()
+        high, total, moment = merged(so2, si2, k)
+        inverse = 1.0 / total
+        mean = moment * inverse
+        fold, label = aux[k, 0:1, :], aux[k, 8:9, :]
+        classes = lax.broadcasted_iota(jnp.int32, (per, LANES), 0) + cls * per
+        onehot = jnp.where(classes.astype(jnp.float32) == label, 1.0, 0.0)
+        res, cur = [], []
+        for s in range(SLOTS):
+            prob = jnp.exp(slot(xtot, k, 0, s) - high[s : s + 1]) * inverse[s : s + 1]
+            res.append(prob - onehot)
+            cur.append(prob * (slot(xtot, k, 1, s) - mean[s : s + 1]))
+        for half, values in enumerate((res, cur)):
+            for s, value in enumerate(values):
+                rsend[k, pl.ds(half * packed + s * per, per), :] = value.astype(jnp.bfloat16)
+        rcopy[k].start()
+        unpack(res, nat, 0, per, fold)
+        unpack(cur, nat, cols, per, fold)
+        place(rown, k)
+
+    def stage_g(k):
+        rcopy[k].wait_recv()
+        fold = auxp[k, 0:1, :]
+        for half in range(2):
+            slots = [slot(rrecv, k, half, s).astype(jnp.float32) for s in range(SLOTS)]
+            unpack(slots, nat, half * cols, per, fold)
+        place(rpeer, k)
+
+    stages = {
+        "a": (stage_a, 0), "b": (stage_b, 1), "c": (stage_c, 2), "o": (stage_o, 1),
+        "d": (stage_d, 4), "e": (stage_e, 5), "f": (stage_f, 6), "g": (stage_g, 8),
+    }
+    keep = pltpu.make_async_copy(ep, epout, lsem.at[3])
+    for step in range(chunks + 9):
+        for name in "abcodefg":
+            run, lag = stages[name]
+            k = step - lag
+            if 0 <= k < chunks:
+                run(k)
+                if name == "c" and k == chunks - 1:
+                    keep.start()
+
+    acopy.wait_send()
+    for copies in (ycopy, xcopy, c1copy, c2copy, pcopy, rcopy):
+        for copy in copies:
+            copy.wait_send()
+    for k in range(chunks):
+        for copy in s1copy[k] + s2copy[k]:
+            copy.wait_send()
+    keep.wait()
+
+
+def product(idx, rown, rpeer, em, ep, grad, hvp):
+    cols = grad.shape[0]
+    total = jnp.dot(rown[...], em[...], preferred_element_type=jnp.float32)
+    total = total + jnp.dot(rpeer[...], ep[...], preferred_element_type=jnp.float32)
+    grad[...] = total[:cols]
+    hvp[...] = total[cols:]
+
+
+def paired(embeddings, fold_ids, labels, weights, direction):
+    rows = embeddings.shape[0]
+    share, cols = weights.shape
+    per = cols // FOLDS
+    packed = 2 * SLOTS * per
+    chunks = -(-rows // LANES)
+    starts = [min(LANES * k, rows - LANES) for k in range(chunks)]
+    both = jnp.stack([fold_ids, labels]).astype(jnp.float32)
+    aux = jnp.stack([both[:, s : s + LANES] for s in starts])
+    aux = jnp.broadcast_to(aux[:, :, None, :], (chunks, 2, 8, LANES)).reshape(chunks, 16, LANES)
+    f32, bf16 = jnp.float32, jnp.bfloat16
+    any_space = pl.BlockSpec(memory_space=pl.ANY)
+    vmem = pl.BlockSpec(memory_space=pltpu.VMEM)
+    dma = pltpu.SemaphoreType.DMA
+    rown, rpeer, ep = pl.pallas_call(
+        exchange,
+        out_shape=(
+            jax.ShapeDtypeStruct((2 * cols, rows), bf16),
+            jax.ShapeDtypeStruct((2 * cols, rows), bf16),
+            jax.ShapeDtypeStruct((rows, share), bf16),
+        ),
+        in_specs=[any_space, any_space, any_space, vmem],
+        out_specs=(vmem, vmem, any_space),
+        scratch_shapes=[
+            pltpu.VMEM((2 * cols, share), bf16),
+            pltpu.VMEM((rows, share), bf16),
+            pltpu.VMEM((rows, share), bf16),
+            pltpu.VMEM((chunks, 16, LANES), f32),
+            pltpu.VMEM((2 * cols, LANES), f32),
+            pltpu.VMEM((chunks, packed, LANES), f32),
+            pltpu.VMEM((chunks, packed, LANES), f32),
+            pltpu.VMEM((chunks, packed, LANES), f32),
+            pltpu.VMEM((chunks, 16, LANES), f32),
+            pltpu.VMEM((chunks, 3, 16, LANES), f32),
+            pltpu.VMEM((chunks, 16, LANES), f32),
+            pltpu.VMEM((chunks, 3, 16, LANES), f32),
+            pltpu.VMEM((chunks, packed, LANES), bf16),
+            pltpu.VMEM((chunks, packed, LANES), bf16),
+            dma((4,)),
+            dma((2,)),
+        ]
+        + [dma((chunks,))] * 10
+        + [dma((chunks, 3))] * 4
+        + [dma((chunks,))] * 2,
+        compiler_params=pltpu.CompilerParams(
+            collective_id=0, has_side_effects=True, vmem_limit_bytes=40 * 2**20
+        ),
+        name="exchange",
+    )(embeddings, weights.T, direction.T, aux)
+
+    tile = 512
+    place = lax.axis_index("dp").astype(jnp.int32).reshape(1) * (share // tile)
+    grad, hvp = pl.pallas_call(
+        product,
+        out_shape=(jax.ShapeDtypeStruct((cols, share), f32),) * 2,
+        grid_spec=pltpu.PrefetchScalarGridSpec(
+            num_scalar_prefetch=1,
+            grid=(share // tile,),
+            in_specs=[
+                pl.BlockSpec((2 * cols, rows), lambda i, s: (0, 0)),
+                pl.BlockSpec((2 * cols, rows), lambda i, s: (0, 0)),
+                pl.BlockSpec((rows, tile), lambda i, s: (0, i + s[0])),
+                pl.BlockSpec((rows, tile), lambda i, s: (0, i)),
+            ],
+            out_specs=(pl.BlockSpec((cols, tile), lambda i, s: (0, i)),) * 2,
+        ),
+        compiler_params=pltpu.CompilerParams(vmem_limit_bytes=32 * 2**20),
+        name="product",
+    )(place, rown, rpeer, embeddings, ep)
+    return grad.T, hvp.T
+
+
 def solution(mesh):
     placed = (P("dp", None), P("dp"), P("dp"), P("dp", "cls"), P("dp", "cls"))
+    body = paired if mesh.shape["dp"] == 2 and mesh.shape["cls"] == 16 else local
     return jax.shard_map(
-        local,
+        body,
         mesh=mesh,
         in_specs=placed,
         out_specs=(P("dp", "cls"), P("dp", "cls")),

time: 460 us -> 79.7 us (0.17)
  waiting for transfers between devices: 283 us -> 0 us
  blocking collectives: 119 us -> 0 us
  Pallas kernels: 0 us -> 72.2 us
  matrix products: 24.2 us -> 0 us
  between operations: 13.9 us -> 0.68 us
  local copies, waits for them, and re-layouts: 17.6 us -> 6.47 us
    psum x1 -> x0, waiting for transfers between devices: 240 us -> none  [local(): lax.psum((lax.dot_general(embeddings, residual_rows, contract, preferred_...]
    pallas_call x0 -> x2, Pallas kernels: none -> 72.2 us  [the longest x1 66.1 us: paired(): pl.pallas_call(exchange, out_shape=(jax.ShapeDtypeStruct((2 * cols, rows)...]
    pmax x1 -> x0, blocking collectives: 61.2 us -> none  [local(): highest = lax.pmax(local_high, 'cls')]
    psum x1 -> x0, blocking collectives: 57.7 us -> none  [local(): lax.psum((jnp.sum(scaled, axis=1), jnp.sum(scaled * tangent, axis=1)), 'c...]
    all_gather x2 -> x0, waiting for transfers between devices: 41.1 us -> none  [the longest x1 41.1 us: local(): lax.all_gather(weights, 'dp', axis=0, tiled=True)]
    dot_general x4 -> x0, matrix products: 24.2 us -> none  [the longest x1 8.03 us: local(): lax.dot_general(embeddings, curvature, contract, preferred_element_type=j...]
    sub x6 -> x0, local copies, waits for them, and re-layouts: 8.25 us -> none  [the longest x2 3.6 us: local(): tangent - mean_tangent[:, None, :]]
    dynamic_slice x1 -> x0, local copies, waits for them, and re-layouts: 5.53 us -> none  [local(): hess_vec = lax.dynamic_slice_in_dim(full_hvp, offset, share, 0)]
  transfers between devices with their start and end apart: 3 -> 0, of which waited for: 2 -> 0; matrix products, arithmetic and copies ran while one was open for 2% -> 0% of each run, Pallas kernels for 0% -> 0%
where the time goes in v1:
time: 79.7 us; the launch traced here: 79.4 us
  Pallas kernels  72.2 us (91%)
  local copies, waits for them, and re-layouts  6.47 us (8%)
    pallas_call x1, Pallas kernels, paired(): pl.pallas_call(exchange, out_shape=(jax.ShapeDtypeStruct((2 * cols, rows)...  66.1 us
    pallas_call x1, Pallas kernels, paired(): pl.pallas_call(product, out_shape=(jax.ShapeDtypeStruct((cols, share), f3...  6.14 us
    unnamed x12, local copies, waits for them, and re-layouts  5 us

profile of v1, /device:TPU:0, one launch (start us, length us, event | category | flops | bytes accessed | tf_op | source)
XLA Modules:
  0.0 79.4 jit_solution(4388657454670187574)
XLA Ops:
  0.6 0.7 stack.27
  1.3 0.7 stack.28
  2.1 0.1 constant_dynamic-update-slice_fusion
  2.2 0.0 copy-start
  2.2 2.3 %copy-done = bf16[576,4096]{1,0:T(8,128)(2,1)S(1)} copy-done((bf16[576,4096]{1,0:T(8,128)(2,1)S(1)}, bf16[576,4096]{1,0:T(8,128)(2,1)}, u32[]{:S(2)}) %copy-start) | copy-done | bytes 4718616
  4.5 0.0 copy-start.2
  4.5 1.3 %copy-done.2 = bf16[2048,320]{0,1:T(8,128)(2,1)S(1)} copy-done((bf16[2048,320]{0,1:T(8,128)(2,1)S(1)}, bf16[2048,320]{0,1:T(8,128)(2,1)}, u32[]{:S(2)}) %copy-start.2) | copy-done | bytes 1310744
  5.8 0.0 copy-start.3
  5.8 1.3 %copy-done.3 = bf16[2048,320]{0,1:T(8,128)(2,1)S(1)} copy-done((bf16[2048,320]{0,1:T(8,128)(2,1)S(1)}, bf16[2048,320]{0,1:T(8,128)(2,1)}, u32[]{:S(2)}) %copy-start.3) | copy-done | bytes 1310744
  7.1 0.0 copy-start.1
  7.1 66.1 %exchange.1 = (bf16[640,576]{1,0:T(8,128)(2,1)S(1)}, bf16[640,576]{1,0:T(8,128)(2,1)S(1)}, bf16[576,2048]{1,0:T(8,128)(2,1)S(1)}) custom-call(bf16[576,4096]{1,0:T(8,128)(2,1)S(1)} %copy-done, bf16[320,2048]{1,0:T(8,128)(2,1)S(1)} %bitcast.27, bf16[320,2048]{1,0:T(8,128)(2,1)S(1)} %bitcast.28, f32[5,16,128]{2,1,0:T(8,128)S(1)} %broadcast_bitcast_fusion.aux), custom_call_target="tpu_custom_call" | custom-call | tf_op jit(solution)/shard_map/exchange/pallas_call | solution.py:323
  73.2 0.0 copy-done.1
  73.2 6.1 %product.1 = (f32[320,2048]{1,0:T(8,128)}, f32[320,2048]{1,0:T(8,128)}) custom-call(s32[1]{0:T(128)} %bitcast.idx, bf16[640,576]{1,0:T(8,128)(2,1)S(1)} %get-tuple-element.7.rown, bf16[640,576]{1,0:T(8,128)(2,1)S(1)} %get-tuple-element.8.rpeer, bf16[576,4096]{1,0:T(8,128)(2,1)S(1)} %copy-done.1, bf16[576,2048]{1,0:T(8,128)(2,1)S(1)} %get-tuple-element.9.ep), custom_call_target="tpu_custom_call" | custom-call | tf_op jit(solution)/shard_map/product/pallas_call | solution.py:361
  (6 shorter events, 0.1 us)
Async XLA Ops:
  2.2 2.3 %copy-start = (bf16[576,4096]{1,0:T(8,128)(2,1)S(1)}, bf16[576,4096]{1,0:T(8,128)(2,1)}, u32[]{:S(2)}) copy-start(bf16[576,4096]{1,0:T(8,128)(2,1)} %em.1) | copy-start | bytes 14155780
  4.5 1.3 %copy-start.2 = (bf16[2048,320]{0,1:T(8,128)(2,1)S(1)}, bf16[2048,320]{0,1:T(8,128)(2,1)}, u32[]{:S(2)}) copy-start(bf16[2048,320]{0,1:T(8,128)(2,1)} %param.8) | copy-start | bytes 3932164
  5.8 1.3 %copy-start.3 = (bf16[2048,320]{0,1:T(8,128)(2,1)S(1)}, bf16[2048,320]{0,1:T(8,128)(2,1)}, u32[]{:S(2)}) copy-start(bf16[2048,320]{0,1:T(8,128)(2,1)} %param.9) | copy-start | bytes 3932164
  7.1 66.1 %copy-start.1 = (bf16[576,4096]{1,0:T(8,128)(2,1)S(1)}, bf16[576,4096]{1,0:T(8,128)(2,1)}, u32[]{:S(2)}) copy-start(bf16[576,4096]{1,0:T(8,128)(2,1)} %em.1) | copy-start | bytes 14155780

commit v2 on v1

--- a/solution.py
+++ b/solution.py
@@ -100,8 +100,8 @@
 
 
 def exchange(
-    e, wt, dt, aux, rown, rpeer, epout,
-    wd, em, ep, auxp, nat, xsend, xrecv, xtot, so1, si1, so2, si2, rsend, rrecv,
+    e, wt, dt, folds, labels, partout, rpeer, epout,
+    part, wd, em, ep, aux, auxp, rown, nat, xsend, xrecv, xtot, so1, si1, so2, si2, rsend, rrecv,
     lsem, asem, ys, yr, xs, xr, c1s, c1r, c2s, c2r, ps, pr, s1s, s1r, s2s, s2r, rs, rr,
 ):
     rows, share = em.shape
@@ -112,6 +112,11 @@
     chunks = xsend.shape[0]
     starts = [min(LANES * k, rows - LANES) for k in range(chunks)]
     pieces = [(LANES * k, min(LANES, rows - LANES * k)) for k in range(chunks)]
+
+    def halved(k):
+        return starts[k] + LANES // 2 == LANES * k
+
+    low = lax.broadcasted_iota(jnp.int32, (per, LANES), 1) < LANES // 2
 
     d = lax.axis_index("dp")
     cls = lax.axis_index("cls")
@@ -134,13 +139,16 @@
             e.at[:, pl.ds(pl.multiple_of(d * share, share), share)], em, lsem.at[2]
         ),
     ]
-    for load in loads:
-        load.start()
-
     barrier = pltpu.get_barrier_semaphore()
     partners = [peer] + [(d, g) for g in group] + [(d, g) for g in zgroup]
     for partner in partners:
         pl.semaphore_signal(barrier, inc=1, device_id=partner, device_id_type=MESH)
+    for load in loads:
+        load.start()
+    for base, values in ((0, folds), (8, labels)):
+        row = values[...].astype(jnp.float32).reshape(1, rows)
+        for k, s in enumerate(starts):
+            aux[k, base : base + 8, :] = jnp.broadcast_to(row[:, s : s + LANES], (8, LANES))
     pl.semaphore_wait(barrier, len(partners))
 
     def remote(src, dst, send, recv, to):
@@ -161,8 +169,11 @@
         xcopy.append(remote(ep.at[r, qa], ep.at[r, qa], xs.at[t], xr.at[t], (d, xn)))
         c1copy.append(remote(ep.at[r, qa], ep.at[r, qa], c1s.at[t], c1r.at[t], (d, core)))
         c2copy.append(remote(ep.at[r, qb], ep.at[r, qb], c2s.at[t], c2r.at[t], (d, core)))
-    pcopy = [remote(xsend.at[k], xrecv.at[k], ps.at[k], pr.at[k], peer) for k in range(chunks)]
-    rcopy = [remote(rsend.at[k], rrecv.at[k], rs.at[k], rr.at[k], peer) for k in range(chunks)]
+    pcopy, rcopy = [], []
+    for k in range(chunks):
+        r = pl.ds(0, packed if halved(k) else 2 * packed)
+        pcopy.append(remote(xsend.at[k, r], xrecv.at[k, r], ps.at[k], pr.at[k], peer))
+        rcopy.append(remote(rsend.at[k, r], rrecv.at[k, r], rs.at[k], rr.at[k], peer))
     s1copy = [
         [remote(so1.at[k], si1.at[k, j], s1s.at[k, j], s1r.at[k, j], (d, g)) for j, g in enumerate(group)]
         for k in range(chunks)
@@ -178,13 +189,26 @@
     for load in loads:
         load.wait()
 
-    def partial_slots(emb, k, fold, out):
+    def partial_slots(emb, k, fold, out, joined):
         nat[...] = lax.dot_general(
             wd[...], emb[pl.ds(starts[k], LANES), :], NT, preferred_element_type=jnp.float32
         )
-        for half in range(2):
-            for s, block in enumerate(pack(nat, half * cols, per, fold)):
-                out[k, pl.ds(half * packed + s * per, per), :] = block
+        store(out, k, [pack(nat, half * cols, per, fold) for half in range(2)], joined)
+
+    def store(out, k, halves, joined):
+        if joined:
+            halves = [
+                [jnp.where(low, pltpu.roll(b, LANES // 2, 1), a) for a, b in zip(*halves)]
+            ]
+        for half, blocks in enumerate(halves):
+            for s, block in enumerate(blocks):
+                out[k, pl.ds(half * packed + s * per, per), :] = block.astype(out.dtype)
+
+    def received(ref, k, half, s):
+        if halved(k):
+            block = slot(ref, k, 0, s).astype(jnp.float32)
+            return pltpu.roll(block, LANES // 2, 1) if half else block
+        return slot(ref, k, half, s).astype(jnp.float32)
 
     def stage_a(t):
         ycopy[t].wait_recv()
@@ -196,14 +220,14 @@
         c2copy[t].start()
 
     def stage_o(k):
-        partial_slots(em, k, aux[k, 0:1, :], xtot)
+        partial_slots(em, k, aux[k, 0:1, :], xtot, False)
 
     def stage_c(k):
         if k == 0:
             acopy.wait_recv()
         c1copy[k].wait_recv()
         c2copy[k].wait_recv()
-        partial_slots(ep, k, auxp[k, 0:1, :], xsend)
+        partial_slots(ep, k, auxp[k, 0:1, :], xsend, halved(k))
         pcopy[k].start()
 
     def slot(ref, k, half, s):
@@ -211,14 +235,16 @@
 
     def stage_d(k):
         pcopy[k].wait_recv()
-        xtot[k] = xtot[k] + xrecv[k]
         for s in range(SLOTS):
-            logit = slot(xtot, k, 0, s)
+            logit = slot(xtot, k, 0, s) + received(xrecv, k, 0, s)
+            tangent = slot(xtot, k, 1, s) + received(xrecv, k, 1, s)
+            xtot[k, pl.ds(s * per, per), :] = logit
+            xtot[k, pl.ds(packed + s * per, per), :] = tangent
             high = jnp.max(logit, axis=0, keepdims=True)
             scaled = jnp.exp(logit - high)
             so1[k, s : s + 1, :] = high
             so1[k, 4 + s : 5 + s, :] = jnp.sum(scaled, axis=0, keepdims=True)
-            so1[k, 8 + s : 9 + s, :] = jnp.sum(scaled * slot(xtot, k, 1, s), axis=0, keepdims=True)
+            so1[k, 8 + s : 9 + s, :] = jnp.sum(scaled * tangent, axis=0, keepdims=True)
         so1[k, 12:16, :] = jnp.zeros((4, LANES), jnp.float32)
         for copy in s1copy[k]:
             copy.start()
@@ -258,10 +284,7 @@
             prob = jnp.exp(slot(xtot, k, 0, s) - high[s : s + 1]) * inverse[s : s + 1]
             res.append(prob - onehot)
             cur.append(prob * (slot(xtot, k, 1, s) - mean[s : s + 1]))
-        for half, values in enumerate((res, cur)):
-            for s, value in enumerate(values):
-                rsend[k, pl.ds(half * packed + s * per, per), :] = value.astype(jnp.bfloat16)
-        rcopy[k].start()
+        store(rsend, k, (res, cur), halved(k))
         unpack(res, nat, 0, per, fold)
         unpack(cur, nat, cols, per, fold)
         place(rown, k)
@@ -270,23 +293,51 @@
         rcopy[k].wait_recv()
         fold = auxp[k, 0:1, :]
         for half in range(2):
-            slots = [slot(rrecv, k, half, s).astype(jnp.float32) for s in range(SLOTS)]
+            slots = [received(rrecv, k, half, s) for s in range(SLOTS)]
             unpack(slots, nat, half * cols, per, fold)
         place(rpeer, k)
 
-    stages = {
-        "a": (stage_a, 0), "b": (stage_b, 1), "c": (stage_c, 2), "o": (stage_o, 1),
-        "d": (stage_d, 4), "e": (stage_e, 5), "f": (stage_f, 6), "g": (stage_g, 8),
-    }
     keep = pltpu.make_async_copy(ep, epout, lsem.at[3])
-    for step in range(chunks + 9):
-        for name in "abcodefg":
-            run, lag = stages[name]
-            k = step - lag
-            if 0 <= k < chunks:
-                run(k)
-                if name == "c" and k == chunks - 1:
-                    keep.start()
+    last = chunks - 1
+    width = 512
+    spans = [pl.ds(i * width, width) for i in range(share // width)]
+    saves = [
+        pltpu.make_async_copy(part.at[:, span], partout.at[:, span], lsem.at[4 + i])
+        for i, span in enumerate(spans)
+    ]
+
+    def own_product(span, at, size):
+        return jnp.dot(
+            rown[:, pl.ds(at, size)], em[pl.ds(at, size), span], preferred_element_type=jnp.float32
+        )
+
+    for step in range(chunks + 2):
+        for stage, lag in ((stage_a, 0), (stage_b, 1), (stage_c, 2), (stage_o, 1)):
+            if 0 <= step - lag < chunks:
+                stage(step - lag)
+    keep.start()
+    for k in range(last - 1):
+        stage_d(k)
+        stage_e(k)
+        stage_f(k)
+    stage_d(last - 1)
+    stage_e(last - 1)
+    stage_d(last)
+    for copy in rcopy[: last - 1]:
+        copy.start()
+    stage_f(last - 1)
+    rcopy[last - 1].start()
+    stage_e(last)
+    for span in spans:
+        part[:, span] = own_product(span, 0, LANES * last)
+    stage_f(last)
+    rcopy[last].start()
+
+    for i, span in enumerate(spans):
+        part[:, span] += own_product(span, LANES * last, rows - LANES * last)
+        saves[i].start()
+    for k in range(chunks):
+        stage_g(k)
 
     acopy.wait_send()
     for copies in (ycopy, xcopy, c1copy, c2copy, pcopy, rcopy):
@@ -296,12 +347,13 @@
         for copy in s1copy[k] + s2copy[k]:
             copy.wait_send()
     keep.wait()
-
-
-def product(idx, rown, rpeer, em, ep, grad, hvp):
+    for save in saves:
+        save.wait()
+
+
+def product(part, rpeer, ep, grad, hvp):
     cols = grad.shape[0]
-    total = jnp.dot(rown[...], em[...], preferred_element_type=jnp.float32)
-    total = total + jnp.dot(rpeer[...], ep[...], preferred_element_type=jnp.float32)
+    total = part[...] + jnp.dot(rpeer[...], ep[...], preferred_element_type=jnp.float32)
     grad[...] = total[:cols]
     hvp[...] = total[cols:]
 
@@ -312,28 +364,27 @@
     per = cols // FOLDS
     packed = 2 * SLOTS * per
     chunks = -(-rows // LANES)
-    starts = [min(LANES * k, rows - LANES) for k in range(chunks)]
-    both = jnp.stack([fold_ids, labels]).astype(jnp.float32)
-    aux = jnp.stack([both[:, s : s + LANES] for s in starts])
-    aux = jnp.broadcast_to(aux[:, :, None, :], (chunks, 2, 8, LANES)).reshape(chunks, 16, LANES)
     f32, bf16 = jnp.float32, jnp.bfloat16
-    any_space = pl.BlockSpec(memory_space=pl.ANY)
+    hbm = pl.BlockSpec(memory_space=pltpu.HBM)
     vmem = pl.BlockSpec(memory_space=pltpu.VMEM)
     dma = pltpu.SemaphoreType.DMA
-    rown, rpeer, ep = pl.pallas_call(
+    part, rpeer, ep = pl.pallas_call(
         exchange,
         out_shape=(
-            jax.ShapeDtypeStruct((2 * cols, rows), bf16),
+            jax.ShapeDtypeStruct((2 * cols, share), f32),
             jax.ShapeDtypeStruct((2 * cols, rows), bf16),
             jax.ShapeDtypeStruct((rows, share), bf16),
         ),
-        in_specs=[any_space, any_space, any_space, vmem],
-        out_specs=(vmem, vmem, any_space),
+        in_specs=[hbm, hbm, hbm, vmem, vmem],
+        out_specs=(hbm, vmem, hbm),
         scratch_shapes=[
+            pltpu.VMEM((2 * cols, share), f32),
             pltpu.VMEM((2 * cols, share), bf16),
             pltpu.VMEM((rows, share), bf16),
             pltpu.VMEM((rows, share), bf16),
             pltpu.VMEM((chunks, 16, LANES), f32),
+            pltpu.VMEM((chunks, 16, LANES), f32),
+            pltpu.VMEM((2 * cols, rows), bf16),
             pltpu.VMEM((2 * cols, LANES), f32),
             pltpu.VMEM((chunks, packed, LANES), f32),
             pltpu.VMEM((chunks, packed, LANES), f32),
@@ -344,37 +395,32 @@
             pltpu.VMEM((chunks, 3, 16, LANES), f32),
             pltpu.VMEM((chunks, packed, LANES), bf16),
             pltpu.VMEM((chunks, packed, LANES), bf16),
-            dma((4,)),
+            dma((4 + share // 512,)),
             dma((2,)),
         ]
         + [dma((chunks,))] * 10
         + [dma((chunks, 3))] * 4
         + [dma((chunks,))] * 2,
         compiler_params=pltpu.CompilerParams(
-            collective_id=0, has_side_effects=True, vmem_limit_bytes=40 * 2**20
+            collective_id=0, has_side_effects=True, vmem_limit_bytes=60 * 2**20
         ),
         name="exchange",
-    )(embeddings, weights.T, direction.T, aux)
+    )(embeddings, weights.T, direction.T, fold_ids, labels)
 
     tile = 512
-    place = lax.axis_index("dp").astype(jnp.int32).reshape(1) * (share // tile)
     grad, hvp = pl.pallas_call(
         product,
         out_shape=(jax.ShapeDtypeStruct((cols, share), f32),) * 2,
-        grid_spec=pltpu.PrefetchScalarGridSpec(
-            num_scalar_prefetch=1,
-            grid=(share // tile,),
-            in_specs=[
-                pl.BlockSpec((2 * cols, rows), lambda i, s: (0, 0)),
-                pl.BlockSpec((2 * cols, rows), lambda i, s: (0, 0)),
-                pl.BlockSpec((rows, tile), lambda i, s: (0, i + s[0])),
-                pl.BlockSpec((rows, tile), lambda i, s: (0, i)),
-            ],
-            out_specs=(pl.BlockSpec((cols, tile), lambda i, s: (0, i)),) * 2,
-        ),
-        compiler_params=pltpu.CompilerParams(vmem_limit_bytes=32 * 2**20),
+        grid=(share // tile,),
+        in_specs=[
+            pl.BlockSpec((2 * cols, tile), lambda i: (0, i)),
+            pl.BlockSpec((2 * cols, rows), lambda i: (0, 0)),
+            pl.BlockSpec((rows, tile), lambda i: (0, i)),
+        ],
+        out_specs=(pl.BlockSpec((cols, tile), lambda i: (0, i)),) * 2,
+        compiler_params=pltpu.CompilerParams(vmem_limit_bytes=60 * 2**20),
         name="product",
-    )(place, rown, rpeer, embeddings, ep)
+    )(part, rpeer, ep)
     return grad.T, hvp.T
 
 

time: 79.7 us -> 81.3 us (1.020)
  Pallas kernels: 72.2 us -> 80.5 us
  local copies, waits for them, and re-layouts: 6.47 us -> 0 us
    pallas_call x1, Pallas kernels: 66.1 us -> 73.4 us  [paired(): pl.pallas_call(exchange, out_shape=(jax.ShapeDtypeStruct((2 * cols, share...]
    unnamed x12 -> x0, local copies, waits for them, and re-layouts: 5 us -> none
    another operation x3 -> x0, local copies, waits for them, and re-layouts: 1.46 us -> none  [the longest x2 1.38 us: paired(): both = jnp.stack([fold_ids, labels]).astype(jnp.float32)]
    pallas_call x1, Pallas kernels: 6.14 us -> 7.1 us  [paired(): pl.pallas_call(product, out_shape=(jax.ShapeDtypeStruct((cols, share), f3...]
where the time goes in v2:
time: 81.3 us; the launch traced here: 81.1 us
  Pallas kernels  80.5 us (99%)
    pallas_call x1, Pallas kernels, paired(): pl.pallas_call(exchange, out_shape=(jax.ShapeDtypeStruct((2 * cols, share...  73.4 us
    pallas_call x1, Pallas kernels, paired(): pl.pallas_call(product, out_shape=(jax.ShapeDtypeStruct((cols, share), f3...  7.1 us

profile of v2, /device:TPU:0, one launch (start us, length us, event | category | flops | bytes accessed | tf_op | source)
XLA Modules:
  0.0 81.1 jit_solution(4286496311657706989)
XLA Ops:
  0.6 73.4 %exchange.1 = (f32[640,2048]{1,0:T(8,128)}, bf16[640,576]{1,0:T(8,128)(2,1)}, bf16[576,2048]{1,0:T(8,128)(2,1)}) custom-call(bf16[576,4096]{1,0:T(8,128)(2,1)} %e.1, bf16[320,2048]{1,0:T(8,128)(2,1)} %bitcast.4, bf16[320,2048]{1,0:T(8,128)(2,1)} %bitcast.5, s32[576]{0:T(1024)} %folds.1, s32[576]{0:T(1024)} %labels.1), custom_call_target="tpu_custom_call" | custom-call | tf_op jit(solution)/shard_map/exchange/pallas_call | solution.py:371
  74.0 7.1 %product.1 = (f32[320,2048]{1,0:T(8,128)}, f32[320,2048]{1,0:T(8,128)}) custom-call(f32[640,2048]{1,0:T(8,128)} %get-tuple-element.7.part, bf16[640,576]{1,0:T(8,128)(2,1)} %get-tuple-element.8.rpeer, bf16[576,2048]{1,0:T(8,128)(2,1)} %get-tuple-element.9.ep), custom_call_target="tpu_custom_call" | custom-call | tf_op jit(solution)/shard_map/product/pallas_call | solution.py:411

commit v3 on v2

--- a/solution.py
+++ b/solution.py
@@ -100,23 +100,23 @@
 
 
 def exchange(
-    e, wt, dt, folds, labels, partout, rpeer, epout,
-    part, wd, em, ep, aux, auxp, rown, nat, xsend, xrecv, xtot, so1, si1, so2, si2, rsend, rrecv,
+    e, wt, dt, folds, labels, partout, rtail, etail,
+    part, wd, ee, aux, auxp, res_all, nat_own, nat_peer, xsend, xrecv, xtot, so1, si1, so2, si2, rsend, rrecv,
     lsem, asem, ys, yr, xs, xr, c1s, c1r, c2s, c2r, ps, pr, s1s, s1r, s2s, s2r, rs, rr,
 ):
-    rows, share = em.shape
+    rows, share = ee.shape[0] // 2, ee.shape[1]
     cols = wt.shape[0]
     per = cols // FOLDS
     packed = SLOTS * per
     quarter = share // 4
     chunks = xsend.shape[0]
-    starts = [min(LANES * k, rows - LANES) for k in range(chunks)]
     pieces = [(LANES * k, min(LANES, rows - LANES * k)) for k in range(chunks)]
 
     def halved(k):
-        return starts[k] + LANES // 2 == LANES * k
-
-    low = lax.broadcasted_iota(jnp.int32, (per, LANES), 1) < LANES // 2
+        return pieces[k][1] < LANES
+
+    last = chunks - 1
+    low = lax.broadcasted_iota(jnp.int32, (1, LANES), 1) < LANES // 2
 
     d = lax.axis_index("dp")
     cls = lax.axis_index("cls")
@@ -135,9 +135,13 @@
     loads = [
         pltpu.make_async_copy(wt, wd.at[pl.ds(0, cols)], lsem.at[0]),
         pltpu.make_async_copy(dt, wd.at[pl.ds(cols, cols)], lsem.at[1]),
+    ] + [
         pltpu.make_async_copy(
-            e.at[:, pl.ds(pl.multiple_of(d * share, share), share)], em, lsem.at[2]
-        ),
+            e.at[pl.ds(at, size), pl.ds(pl.multiple_of(d * share, share), share)],
+            ee.at[pl.ds(2 * at, size)],
+            lsem.at[2 + t],
+        )
+        for t, (at, size) in enumerate(pieces)
     ]
     barrier = pltpu.get_barrier_semaphore()
     partners = [peer] + [(d, g) for g in group] + [(d, g) for g in zgroup]
@@ -147,8 +151,9 @@
         load.start()
     for base, values in ((0, folds), (8, labels)):
         row = values[...].astype(jnp.float32).reshape(1, rows)
-        for k, s in enumerate(starts):
-            aux[k, base : base + 8, :] = jnp.broadcast_to(row[:, s : s + LANES], (8, LANES))
+        for k, (at, size) in enumerate(pieces):
+            part_row = jnp.concatenate([row[:, at : at + size]] * (LANES // size), axis=1)
+            aux[k, base : base + 8, :] = jnp.broadcast_to(part_row, (8, LANES))
     pl.semaphore_wait(barrier, len(partners))
 
     def remote(src, dst, send, recv, to):
@@ -164,11 +169,11 @@
     acopy = remote(aux, auxp, asem.at[0], asem.at[1], peer)
     ycopy, xcopy, c1copy, c2copy = [], [], [], []
     for t, (at, size) in enumerate(pieces):
-        r = pl.ds(at, size)
-        ycopy.append(remote(e.at[r, qs], ep.at[r, qa], ys.at[t], yr.at[t], peer))
-        xcopy.append(remote(ep.at[r, qa], ep.at[r, qa], xs.at[t], xr.at[t], (d, xn)))
-        c1copy.append(remote(ep.at[r, qa], ep.at[r, qa], c1s.at[t], c1r.at[t], (d, core)))
-        c2copy.append(remote(ep.at[r, qb], ep.at[r, qb], c2s.at[t], c2r.at[t], (d, core)))
+        r = pl.ds(2 * at + size, size)
+        ycopy.append(remote(e.at[pl.ds(at, size), qs], ee.at[r, qa], ys.at[t], yr.at[t], peer))
+        xcopy.append(remote(ee.at[r, qa], ee.at[r, qa], xs.at[t], xr.at[t], (d, xn)))
+        c1copy.append(remote(ee.at[r, qa], ee.at[r, qa], c1s.at[t], c1r.at[t], (d, core)))
+        c2copy.append(remote(ee.at[r, qb], ee.at[r, qb], c2s.at[t], c2r.at[t], (d, core)))
     pcopy, rcopy = [], []
     for k in range(chunks):
         r = pl.ds(0, packed if halved(k) else 2 * packed)
@@ -186,28 +191,22 @@
     acopy.start()
     for copy in ycopy:
         copy.start()
-    for load in loads:
-        load.wait()
-
-    def partial_slots(emb, k, fold, out, joined):
-        nat[...] = lax.dot_general(
-            wd[...], emb[pl.ds(starts[k], LANES), :], NT, preferred_element_type=jnp.float32
-        )
-        store(out, k, [pack(nat, half * cols, per, fold) for half in range(2)], joined)
-
-    def store(out, k, halves, joined):
-        if joined:
-            halves = [
-                [jnp.where(low, pltpu.roll(b, LANES // 2, 1), a) for a, b in zip(*halves)]
-            ]
+
+    def store(out, k, halves, first):
+        if halved(k):
+            joined = []
+            for x0, x1 in zip(*halves):
+                x1 = pltpu.roll(x1, LANES // 2, 1)
+                joined.append(jnp.where(low, x0, x1) if first else jnp.where(low, x1, x0))
+            halves = [joined]
         for half, blocks in enumerate(halves):
             for s, block in enumerate(blocks):
                 out[k, pl.ds(half * packed + s * per, per), :] = block.astype(out.dtype)
 
-    def received(ref, k, half, s):
+    def received(ref, k, half, s, moved):
         if halved(k):
             block = slot(ref, k, 0, s).astype(jnp.float32)
-            return pltpu.roll(block, LANES // 2, 1) if half else block
+            return pltpu.roll(block, LANES // 2, 1) if half == moved else block
         return slot(ref, k, half, s).astype(jnp.float32)
 
     def stage_a(t):
@@ -219,16 +218,27 @@
         xcopy[t].wait_recv()
         c2copy[t].start()
 
-    def stage_o(k):
-        partial_slots(em, k, aux[k, 0:1, :], xtot, False)
-
     def stage_c(k):
         if k == 0:
             acopy.wait_recv()
+            loads[0].wait()
+            loads[1].wait()
+        loads[2 + k].wait()
         c1copy[k].wait_recv()
         c2copy[k].wait_recv()
-        partial_slots(ep, k, auxp[k, 0:1, :], xsend, halved(k))
+        at, size = pieces[k]
+        both = lax.dot_general(
+            wd[...], ee[pl.ds(2 * at, 2 * size), :], NT, preferred_element_type=jnp.float32
+        )
+        nat_own[...] = both[:, :LANES]
+        nat_peer[...] = both[:, -LANES:]
+        fold = auxp[k, 0:1, :]
+        store(xsend, k, [pack(nat_peer, half * cols, per, fold) for half in range(2)], False)
         pcopy[k].start()
+        fold = aux[k, 0:1, :]
+        for half in range(2):
+            for s, block in enumerate(pack(nat_own, half * cols, per, fold)):
+                xtot[k, pl.ds(half * packed + s * per, per), :] = block
 
     def slot(ref, k, half, s):
         return ref[k, pl.ds(half * packed + s * per, per), :]
@@ -236,8 +246,8 @@
     def stage_d(k):
         pcopy[k].wait_recv()
         for s in range(SLOTS):
-            logit = slot(xtot, k, 0, s) + received(xrecv, k, 0, s)
-            tangent = slot(xtot, k, 1, s) + received(xrecv, k, 1, s)
+            logit = slot(xtot, k, 0, s) + received(xrecv, k, 0, s, 0)
+            tangent = slot(xtot, k, 1, s) + received(xrecv, k, 1, s, 0)
             xtot[k, pl.ds(s * per, per), :] = logit
             xtot[k, pl.ds(packed + s * per, per), :] = tangent
             high = jnp.max(logit, axis=0, keepdims=True)
@@ -262,13 +272,6 @@
         so2[k, 12:16, :] = jnp.zeros((4, LANES), jnp.float32)
         for copy in s2copy[k]:
             copy.start()
-
-    def place(out, k):
-        keep = starts[k] - LANES * k
-        if keep:
-            out[:, pl.ds(LANES * k, LANES + keep)] = nat[:, -keep:].astype(jnp.bfloat16)
-        else:
-            out[:, pl.ds(LANES * k, LANES)] = nat[...].astype(jnp.bfloat16)
 
     def stage_f(k):
         for copy in s2copy[k]:
@@ -284,35 +287,43 @@
             prob = jnp.exp(slot(xtot, k, 0, s) - high[s : s + 1]) * inverse[s : s + 1]
             res.append(prob - onehot)
             cur.append(prob * (slot(xtot, k, 1, s) - mean[s : s + 1]))
-        store(rsend, k, (res, cur), halved(k))
-        unpack(res, nat, 0, per, fold)
-        unpack(cur, nat, cols, per, fold)
-        place(rown, k)
+        store(rsend, k, (res, cur), True)
+        unpack(res, nat_own, 0, per, fold)
+        unpack(cur, nat_own, cols, per, fold)
+        if k < last:
+            res_all[:, pl.ds(2 * LANES * k, LANES)] = nat_own[...].astype(jnp.bfloat16)
 
     def stage_g(k):
         rcopy[k].wait_recv()
         fold = auxp[k, 0:1, :]
         for half in range(2):
-            slots = [received(rrecv, k, half, s) for s in range(SLOTS)]
-            unpack(slots, nat, half * cols, per, fold)
-        place(rpeer, k)
-
-    keep = pltpu.make_async_copy(ep, epout, lsem.at[3])
-    last = chunks - 1
+            slots = [received(rrecv, k, half, s, 1) for s in range(SLOTS)]
+            unpack(slots, nat_peer, half * cols, per, fold)
+        if k == last:
+            tile = jnp.where(low, nat_own[...], pltpu.roll(nat_peer[...], LANES // 2, 1))
+            rtail[:, LANES:] = tile.astype(jnp.bfloat16)
+        elif k == last - 1:
+            rtail[:, :LANES] = nat_peer[...].astype(jnp.bfloat16)
+        else:
+            res_all[:, pl.ds(2 * LANES * k + LANES, LANES)] = nat_peer[...].astype(jnp.bfloat16)
+
+    near = res_all.shape[1]
+    keep = pltpu.make_async_copy(ee.at[pl.ds(near, 2 * rows - near)], etail, lsem.at[2 + chunks])
     width = 512
     spans = [pl.ds(i * width, width) for i in range(share // width)]
     saves = [
-        pltpu.make_async_copy(part.at[:, span], partout.at[:, span], lsem.at[4 + i])
+        pltpu.make_async_copy(part.at[:, span], partout.at[:, span], lsem.at[3 + chunks + i])
         for i, span in enumerate(spans)
     ]
 
     def own_product(span, at, size):
         return jnp.dot(
-            rown[:, pl.ds(at, size)], em[pl.ds(at, size), span], preferred_element_type=jnp.float32
+            res_all[:, pl.ds(at, size)], ee[pl.ds(at, size), span],
+            preferred_element_type=jnp.float32,
         )
 
     for step in range(chunks + 2):
-        for stage, lag in ((stage_a, 0), (stage_b, 1), (stage_c, 2), (stage_o, 1)):
+        for stage, lag in ((stage_a, 0), (stage_b, 1), (stage_c, 2)):
             if 0 <= step - lag < chunks:
                 stage(step - lag)
     keep.start()
@@ -328,16 +339,21 @@
     stage_f(last - 1)
     rcopy[last - 1].start()
     stage_e(last)
-    for span in spans:
-        part[:, span] = own_product(span, 0, LANES * last)
     stage_f(last)
     rcopy[last].start()
 
+    stage_g(0)
+    stage_g(1)
+    half = 4 * LANES
+    for span in spans:
+        part[:, span] = own_product(span, 0, half)
+    for k in range(2, last - 1):
+        stage_g(k)
     for i, span in enumerate(spans):
-        part[:, span] += own_product(span, LANES * last, rows - LANES * last)
+        part[:, span] += own_product(span, half, near - half)
         saves[i].start()
-    for k in range(chunks):
-        stage_g(k)
+    stage_g(last - 1)
+    stage_g(last)
 
     acopy.wait_send()
     for copies in (ycopy, xcopy, c1copy, c2copy, pcopy, rcopy):
@@ -351,9 +367,9 @@
         save.wait()
 
 
-def product(part, rpeer, ep, grad, hvp):
+def product(part, rtail, etail, grad, hvp):
     cols = grad.shape[0]
-    total = part[...] + jnp.dot(rpeer[...], ep[...], preferred_element_type=jnp.float32)
+    total = part[...] + jnp.dot(rtail[...], etail[...], preferred_element_type=jnp.float32)
     grad[...] = total[:cols]
     hvp[...] = total[cols:]
 
@@ -368,23 +384,23 @@
     hbm = pl.BlockSpec(memory_space=pltpu.HBM)
     vmem = pl.BlockSpec(memory_space=pltpu.VMEM)
     dma = pltpu.SemaphoreType.DMA
-    part, rpeer, ep = pl.pallas_call(
+    part, rtail, etail = pl.pallas_call(
         exchange,
         out_shape=(
             jax.ShapeDtypeStruct((2 * cols, share), f32),
-            jax.ShapeDtypeStruct((2 * cols, rows), bf16),
-            jax.ShapeDtypeStruct((rows, share), bf16),
+            jax.ShapeDtypeStruct((2 * cols, 2 * LANES), bf16),
+            jax.ShapeDtypeStruct((2 * LANES, share), bf16),
         ),
         in_specs=[hbm, hbm, hbm, vmem, vmem],
         out_specs=(hbm, vmem, hbm),
         scratch_shapes=[
             pltpu.VMEM((2 * cols, share), f32),
             pltpu.VMEM((2 * cols, share), bf16),
-            pltpu.VMEM((rows, share), bf16),
-            pltpu.VMEM((rows, share), bf16),
+            pltpu.VMEM((2 * rows, share), bf16),
             pltpu.VMEM((chunks, 16, LANES), f32),
             pltpu.VMEM((chunks, 16, LANES), f32),
-            pltpu.VMEM((2 * cols, rows), bf16),
+            pltpu.VMEM((2 * cols, 2 * rows - 2 * LANES), bf16),
+            pltpu.VMEM((2 * cols, LANES), f32),
             pltpu.VMEM((2 * cols, LANES), f32),
             pltpu.VMEM((chunks, packed, LANES), f32),
             pltpu.VMEM((chunks, packed, LANES), f32),
@@ -395,7 +411,7 @@
             pltpu.VMEM((chunks, 3, 16, LANES), f32),
             pltpu.VMEM((chunks, packed, LANES), bf16),
             pltpu.VMEM((chunks, packed, LANES), bf16),
-            dma((4 + share // 512,)),
+            dma((3 + chunks + share // 512,)),
             dma((2,)),
         ]
         + [dma((chunks,))] * 10
@@ -414,13 +430,13 @@
         grid=(share // tile,),
         in_specs=[
             pl.BlockSpec((2 * cols, tile), lambda i: (0, i)),
-            pl.BlockSpec((2 * cols, rows), lambda i: (0, 0)),
-            pl.BlockSpec((rows, tile), lambda i: (0, i)),
+            pl.BlockSpec((2 * cols, 2 * LANES), lambda i: (0, 0)),
+            pl.BlockSpec((2 * LANES, tile), lambda i: (0, i)),
         ],
         out_specs=(pl.BlockSpec((cols, tile), lambda i: (0, i)),) * 2,
         compiler_params=pltpu.CompilerParams(vmem_limit_bytes=60 * 2**20),
         name="product",
-    )(part, rpeer, ep)
+    )(part, rtail, etail)
     return grad.T, hvp.T
 
 

time: 81.3 us -> 75.9 us (0.934)
  Pallas kernels: 80.5 us -> 75.1 us
    pallas_call x1, Pallas kernels: 73.4 us -> 69.3 us  [paired(): pl.pallas_call(exchange, out_shape=(jax.ShapeDtypeStruct((2 * cols, share...]
    pallas_call x1, Pallas kernels: 7.1 us -> 5.8 us  [paired(): pl.pallas_call(product, out_shape=(jax.ShapeDtypeStruct((cols, share), f3...]
where the time goes in v3:
time: 75.9 us; the launch traced here: 75.7 us
  Pallas kernels  75.1 us (99%)
    pallas_call x1, Pallas kernels, paired(): pl.pallas_call(exchange, out_shape=(jax.ShapeDtypeStruct((2 * cols, share...  69.3 us
    pallas_call x1, Pallas kernels, paired(): pl.pallas_call(product, out_shape=(jax.ShapeDtypeStruct((cols, share), f3...  5.8 us

profile of v3, /device:TPU:0, one launch (start us, length us, event | category | flops | bytes accessed | tf_op | source)
XLA Modules:
  0.0 75.7 jit_solution(5413069079250425900)
XLA Ops:
  0.6 69.3 %exchange.1 = (f32[640,2048]{1,0:T(8,128)}, bf16[640,256]{1,0:T(8,128)(2,1)}, bf16[256,2048]{1,0:T(8,128)(2,1)}) custom-call(bf16[576,4096]{1,0:T(8,128)(2,1)} %e.1, bf16[320,2048]{1,0:T(8,128)(2,1)} %bitcast.4, bf16[320,2048]{1,0:T(8,128)(2,1)} %bitcast.5, s32[576]{0:T(1024)} %folds.1, s32[576]{0:T(1024)} %labels.1), custom_call_target="tpu_custom_call" | custom-call | tf_op jit(solution)/shard_map/exchange/pallas_call | solution.py:387
  69.9 5.8 %product.1 = (f32[320,2048]{1,0:T(8,128)}, f32[320,2048]{1,0:T(8,128)}) custom-call(f32[640,2048]{1,0:T(8,128)} %get-tuple-element.7.part, bf16[640,256]{1,0:T(8,128)(2,1)} %get-tuple-element.8.rtail, bf16[256,2048]{1,0:T(8,128)(2,1)} %get-tuple-element.9.etail), custom_call_target="tpu_custom_call" | custom-call | tf_op jit(solution)/shard_map/product/pallas_call | solution.py:427

commit v4 on v3

--- a/solution.py
+++ b/solution.py
@@ -327,20 +327,18 @@
             if 0 <= step - lag < chunks:
                 stage(step - lag)
     keep.start()
-    for k in range(last - 1):
-        stage_d(k)
-        stage_e(k)
-        stage_f(k)
-    stage_d(last - 1)
-    stage_e(last - 1)
-    stage_d(last)
-    for copy in rcopy[: last - 1]:
-        copy.start()
-    stage_f(last - 1)
-    rcopy[last - 1].start()
-    stage_e(last)
-    stage_f(last)
-    rcopy[last].start()
+    for step in range(chunks + 2):
+        if step <= last:
+            stage_d(step)
+        if step == last:
+            for copy in rcopy[: last - 2]:
+                copy.start()
+        if 0 <= step - 1 <= last:
+            stage_e(step - 1)
+        if 0 <= step - 2 <= last:
+            stage_f(step - 2)
+            if step - 2 >= last - 2:
+                rcopy[step - 2].start()
 
     stage_g(0)
     stage_g(1)

time: 75.9 us -> 71.2 us (0.938)
  Pallas kernels: 75.1 us -> 70.4 us
    pallas_call x1, Pallas kernels: 69.3 us -> 64.6 us  [paired(): pl.pallas_call(exchange, out_shape=(jax.ShapeDtypeStruct((2 * cols, share...]
where the time goes in v4:
time: 71.2 us; the launch traced here: 71.1 us
  Pallas kernels  70.4 us (99%)
    pallas_call x1, Pallas kernels, paired(): pl.pallas_call(exchange, out_shape=(jax.ShapeDtypeStruct((2 * cols, share...  64.6 us
    pallas_call x1, Pallas kernels, paired(): pl.pallas_call(product, out_shape=(jax.ShapeDtypeStruct((cols, share), f3...  5.8 us

profile of v4, /device:TPU:0, one launch (start us, length us, event | category | flops | bytes accessed | tf_op | source)
XLA Modules:
  0.0 71.1 jit_solution(6965195912008012231)
XLA Ops:
  0.6 64.6 %exchange.1 = (f32[640,2048]{1,0:T(8,128)}, bf16[640,256]{1,0:T(8,128)(2,1)}, bf16[256,2048]{1,0:T(8,128)(2,1)}) custom-call(bf16[576,4096]{1,0:T(8,128)(2,1)} %e.1, bf16[320,2048]{1,0:T(8,128)(2,1)} %bitcast.4, bf16[320,2048]{1,0:T(8,128)(2,1)} %bitcast.5, s32[576]{0:T(1024)} %folds.1, s32[576]{0:T(1024)} %labels.1), custom_call_target="tpu_custom_call" | custom-call | tf_op jit(solution)/shard_map/exchange/pallas_call | solution.py:385
  65.3 5.8 %product.1 = (f32[320,2048]{1,0:T(8,128)}, f32[320,2048]{1,0:T(8,128)}) custom-call(f32[640,2048]{1,0:T(8,128)} %get-tuple-element.7.part, bf16[640,256]{1,0:T(8,128)(2,1)} %get-tuple-element.8.rtail, bf16[256,2048]{1,0:T(8,128)(2,1)} %get-tuple-element.9.etail), custom_call_target="tpu_custom_call" | custom-call | tf_op jit(solution)/shard_map/product/pallas_call | solution.py:425

commit v5 on v4

--- a/solution.py
+++ b/solution.py
@@ -102,13 +102,13 @@
 def exchange(
     e, wt, dt, folds, labels, partout, rtail, etail,
     part, wd, ee, aux, auxp, res_all, nat_own, nat_peer, xsend, xrecv, xtot, so1, si1, so2, si2, rsend, rrecv,
-    lsem, asem, ys, yr, xs, xr, c1s, c1r, c2s, c2r, ps, pr, s1s, s1r, s2s, s2r, rs, rr,
+    lsem, asem, hs, hr, ps, pr, s1s, s1r, s2s, s2r, rs, rr,
 ):
     rows, share = ee.shape[0] // 2, ee.shape[1]
     cols = wt.shape[0]
     per = cols // FOLDS
     packed = SLOTS * per
-    quarter = share // 4
+    eighth = share // 8
     chunks = xsend.shape[0]
     pieces = [(LANES * k, min(LANES, rows - LANES * k)) for k in range(chunks)]
 
@@ -162,18 +162,33 @@
             device_id=to, device_id_type=MESH,
         )
 
-    qa = pl.ds(pl.multiple_of(q * quarter, quarter), quarter)
-    qb = pl.ds(pl.multiple_of((q + 2 - 4 * x) * quarter, quarter), quarter)
-    qs = pl.ds(pl.multiple_of(other * share + q * quarter, quarter), quarter)
+    zz = z % 2
+    zn = cls + 4 - 8 * zz
+    p = 4 * zz + q
+
+    def piece(index, base=0):
+        return pl.ds(pl.multiple_of(base + index * eighth, eighth), eighth)
+
+    px, pz = p + 2 - 4 * x, p + 4 - 8 * zz
+    pd = px + 4 - 8 * zz
+    pf = (1 - c) * px + c * pz
+    to_diag = (1 - c) * zn + c * xn
 
     acopy = remote(aux, auxp, asem.at[0], asem.at[1], peer)
-    ycopy, xcopy, c1copy, c2copy = [], [], [], []
+    hops = []
     for t, (at, size) in enumerate(pieces):
         r = pl.ds(2 * at + size, size)
-        ycopy.append(remote(e.at[pl.ds(at, size), qs], ee.at[r, qa], ys.at[t], yr.at[t], peer))
-        xcopy.append(remote(ee.at[r, qa], ee.at[r, qa], xs.at[t], xr.at[t], (d, xn)))
-        c1copy.append(remote(ee.at[r, qa], ee.at[r, qa], c1s.at[t], c1r.at[t], (d, core)))
-        c2copy.append(remote(ee.at[r, qb], ee.at[r, qb], c2s.at[t], c2r.at[t], (d, core)))
+        routes = [(p, xn), (p, zn), (p, core), (pf, to_diag), (px, core), (pz, core), (pd, core)]
+        hop = [
+            remote(
+                e.at[pl.ds(at, size), piece(p, other * share)], ee.at[r, piece(p)],
+                hs.at[0, t], hr.at[0, t], peer,
+            )
+        ]
+        for j, (index, to) in enumerate(routes):
+            block = ee.at[r, piece(index)]
+            hop.append(remote(block, block, hs.at[j + 1, t], hr.at[j + 1, t], (d, to)))
+        hops.append(hop)
     pcopy, rcopy = [], []
     for k in range(chunks):
         r = pl.ds(0, packed if halved(k) else 2 * packed)
@@ -189,8 +204,8 @@
     ]
 
     acopy.start()
-    for copy in ycopy:
-        copy.start()
+    for hop in hops:
+        hop[0].start()
 
     def store(out, k, halves, first):
         if halved(k):
@@ -210,13 +225,19 @@
         return slot(ref, k, half, s).astype(jnp.float32)
 
     def stage_a(t):
-        ycopy[t].wait_recv()
-        xcopy[t].start()
-        c1copy[t].start()
+        hops[t][0].wait_recv()
+        for j in (1, 2, 3):
+            hops[t][j].start()
 
     def stage_b(t):
-        xcopy[t].wait_recv()
-        c2copy[t].start()
+        hops[t][1].wait_recv()
+        hops[t][2].wait_recv()
+        for j in (4, 5, 6):
+            hops[t][j].start()
+
+    def stage_x(t):
+        hops[t][4].wait_recv()
+        hops[t][7].start()
 
     def stage_c(k):
         if k == 0:
@@ -224,8 +245,8 @@
             loads[0].wait()
             loads[1].wait()
         loads[2 + k].wait()
-        c1copy[k].wait_recv()
-        c2copy[k].wait_recv()
+        for j in (3, 5, 6, 7):
+            hops[k][j].wait_recv()
         at, size = pieces[k]
         both = lax.dot_general(
             wd[...], ee[pl.ds(2 * at, 2 * size), :], NT, preferred_element_type=jnp.float32
@@ -322,8 +343,8 @@
             preferred_element_type=jnp.float32,
         )
 
-    for step in range(chunks + 2):
-        for stage, lag in ((stage_a, 0), (stage_b, 1), (stage_c, 2)):
+    for step in range(chunks + 3):
+        for stage, lag in ((stage_a, 0), (stage_b, 1), (stage_x, 2), (stage_c, 3)):
             if 0 <= step - lag < chunks:
                 stage(step - lag)
     keep.start()
@@ -354,7 +375,7 @@
     stage_g(last)
 
     acopy.wait_send()
-    for copies in (ycopy, xcopy, c1copy, c2copy, pcopy, rcopy):
+    for copies in hops + [pcopy, rcopy]:
         for copy in copies:
             copy.wait_send()
     for k in range(chunks):
@@ -412,7 +433,8 @@
             dma((3 + chunks + share // 512,)),
             dma((2,)),
         ]
-        + [dma((chunks,))] * 10
+        + [dma((8, chunks))] * 2
+        + [dma((chunks,))] * 2
         + [dma((chunks, 3))] * 4
         + [dma((chunks,))] * 2,
         compiler_params=pltpu.CompilerParams(

time: 71.2 us -> 71.7 us (level)
  no operation moved by 1% of the time
where the time goes in v5:
time: 71.7 us; the launch traced here: 71.6 us
  Pallas kernels  70.9 us (99%)
    pallas_call x1, Pallas kernels, paired(): pl.pallas_call(exchange, out_shape=(jax.ShapeDtypeStruct((2 * cols, share...  65.1 us
    pallas_call x1, Pallas kernels, paired(): pl.pallas_call(product, out_shape=(jax.ShapeDtypeStruct((cols, share), f3...  5.8 us

profile of v5, /device:TPU:0, one launch (start us, length us, event | category | flops | bytes accessed | tf_op | source)
XLA Modules:
  0.0 71.6 jit_solution(13126780393070443332)
XLA Ops:
  0.6 65.1 %exchange.1 = (f32[640,2048]{1,0:T(8,128)}, bf16[640,256]{1,0:T(8,128)(2,1)}, bf16[256,2048]{1,0:T(8,128)(2,1)}) custom-call(bf16[576,4096]{1,0:T(8,128)(2,1)} %e.1, bf16[320,2048]{1,0:T(8,128)(2,1)} %bitcast.4, bf16[320,2048]{1,0:T(8,128)(2,1)} %bitcast.5, s32[576]{0:T(1024)} %folds.1, s32[576]{0:T(1024)} %labels.1), custom_call_target="tpu_custom_call" | custom-call | tf_op jit(solution)/shard_map/exchange/pallas_call | solution.py:406
  65.8 5.8 %product.1 = (f32[320,2048]{1,0:T(8,128)}, f32[320,2048]{1,0:T(8,128)}) custom-call(f32[640,2048]{1,0:T(8,128)} %get-tuple-element.7.part, bf16[640,256]{1,0:T(8,128)(2,1)} %get-tuple-element.8.rtail, bf16[256,2048]{1,0:T(8,128)(2,1)} %get-tuple-element.9.etail), custom_call_target="tpu_custom_call" | custom-call | tf_op jit(solution)/shard_map/product/pallas_call | solution.py:447

commit v6 on v5

--- a/solution.py
+++ b/solution.py
@@ -348,25 +348,21 @@
             if 0 <= step - lag < chunks:
                 stage(step - lag)
     keep.start()
+    half = 2 * LANES
     for step in range(chunks + 2):
         if step <= last:
             stage_d(step)
-        if step == last:
-            for copy in rcopy[: last - 2]:
-                copy.start()
         if 0 <= step - 1 <= last:
             stage_e(step - 1)
         if 0 <= step - 2 <= last:
             stage_f(step - 2)
-            if step - 2 >= last - 2:
-                rcopy[step - 2].start()
-
-    stage_g(0)
-    stage_g(1)
-    half = 4 * LANES
-    for span in spans:
-        part[:, span] = own_product(span, 0, half)
-    for k in range(2, last - 1):
+            rcopy[step - 2].start()
+        if step == last - 1:
+            stage_g(0)
+            for span in spans:
+                part[:, span] = own_product(span, 0, half)
+
+    for k in range(1, last - 1):
         stage_g(k)
     for i, span in enumerate(spans):
         part[:, span] += own_product(span, half, near - half)
@@ -443,7 +439,7 @@
         name="exchange",
     )(embeddings, weights.T, direction.T, fold_ids, labels)
 
-    tile = 512
+    tile = 256
     grad, hvp = pl.pallas_call(
         product,
         out_shape=(jax.ShapeDtypeStruct((cols, share), f32),) * 2,

time: 71.7 us -> 75.3 us (1.050)
  Pallas kernels: 70.9 us -> 74.3 us
    pallas_call x1, Pallas kernels: 5.8 us -> 8.45 us  [paired(): pl.pallas_call(product, out_shape=(jax.ShapeDtypeStruct((cols, share), f3...]
    pallas_call x1, Pallas kernels: 65.1 us -> 65.9 us  [paired(): pl.pallas_call(exchange, out_shape=(jax.ShapeDtypeStruct((2 * cols, share...]
where the time goes in v6:
time: 75.3 us; the launch traced here: 75 us
  Pallas kernels  74.3 us (99%)
    pallas_call x1, Pallas kernels, paired(): pl.pallas_call(exchange, out_shape=(jax.ShapeDtypeStruct((2 * cols, share...  65.9 us
    pallas_call x1, Pallas kernels, paired(): pl.pallas_call(product, out_shape=(jax.ShapeDtypeStruct((cols, share), f3...  8.45 us

profile of v6, /device:TPU:0, one launch (start us, length us, event | category | flops | bytes accessed | tf_op | source)
XLA Modules:
  0.0 75.0 jit_solution(11637701139599438587)
XLA Ops:
  0.6 65.9 %exchange.1 = (f32[640,2048]{1,0:T(8,128)}, bf16[640,256]{1,0:T(8,128)(2,1)}, bf16[256,2048]{1,0:T(8,128)(2,1)}) custom-call(bf16[576,4096]{1,0:T(8,128)(2,1)} %e.1, bf16[320,2048]{1,0:T(8,128)(2,1)} %bitcast.4, bf16[320,2048]{1,0:T(8,128)(2,1)} %bitcast.5, s32[576]{0:T(1024)} %folds.1, s32[576]{0:T(1024)} %labels.1), custom_call_target="tpu_custom_call" | custom-call | tf_op jit(solution)/shard_map/exchange/pallas_call | solution.py:402
  66.5 8.5 %product.1 = (f32[320,2048]{1,0:T(8,128)}, f32[320,2048]{1,0:T(8,128)}) custom-call(f32[640,2048]{1,0:T(8,128)} %get-tuple-element.7.part, bf16[640,256]{1,0:T(8,128)(2,1)} %get-tuple-element.8.rtail, bf16[256,2048]{1,0:T(8,128)(2,1)} %get-tuple-element.9.etail), custom_call_target="tpu_custom_call" | custom-call | tf_op jit(solution)/shard_map/product/pallas_call | solution.py:443

commit v7 on v4

--- a/solution.py
+++ b/solution.py
@@ -366,10 +366,10 @@
 
 
 def product(part, rtail, etail, grad, hvp):
-    cols = grad.shape[0]
-    total = part[...] + jnp.dot(rtail[...], etail[...], preferred_element_type=jnp.float32)
-    grad[...] = total[:cols]
-    hvp[...] = total[cols:]
+    for half, out in enumerate((grad, hvp)):
+        out[...] = part[half] + jnp.dot(
+            rtail[half], etail[...], preferred_element_type=jnp.float32
+        )
 
 
 def paired(embeddings, fold_ids, labels, weights, direction):
@@ -421,20 +421,20 @@
         name="exchange",
     )(embeddings, weights.T, direction.T, fold_ids, labels)
 
-    tile = 512
+    block = cols // 4
     grad, hvp = pl.pallas_call(
         product,
         out_shape=(jax.ShapeDtypeStruct((cols, share), f32),) * 2,
-        grid=(share // tile,),
+        grid=(cols // block,),
         in_specs=[
-            pl.BlockSpec((2 * cols, tile), lambda i: (0, i)),
-            pl.BlockSpec((2 * cols, 2 * LANES), lambda i: (0, 0)),
-            pl.BlockSpec((2 * LANES, tile), lambda i: (0, i)),
+            pl.BlockSpec((2, block, share), lambda i: (0, i, 0)),
+            pl.BlockSpec((2, block, 2 * LANES), lambda i: (0, i, 0)),
+            pl.BlockSpec((2 * LANES, share), lambda i: (0, 0)),
         ],
-        out_specs=(pl.BlockSpec((cols, tile), lambda i: (0, i)),) * 2,
+        out_specs=(pl.BlockSpec((block, share), lambda i: (i, 0)),) * 2,
         compiler_params=pltpu.CompilerParams(vmem_limit_bytes=60 * 2**20),
         name="product",
-    )(part, rtail, etail)
+    )(part.reshape(2, cols, share), rtail.reshape(2, cols, 2 * LANES), etail)
     return grad.T, hvp.T
 
 

time: 71.2 us -> 71.6 us (level)
  no operation moved by 1% of the time
where the time goes in v7:
time: 71.6 us; the launch traced here: 71.4 us
  Pallas kernels  70.8 us (99%)
    pallas_call x1, Pallas kernels, paired(): pl.pallas_call(exchange, out_shape=(jax.ShapeDtypeStruct((2 * cols, share...  64.6 us
    pallas_call x1, Pallas kernels, paired(): pl.pallas_call(product, out_shape=(jax.ShapeDtypeStruct((cols, share), f3...  6.19 us

profile of v7, /device:TPU:0, one launch (start us, length us, event | category | flops | bytes accessed | tf_op | source)
XLA Modules:
  0.0 71.4 jit_solution(3111297184979809145)
XLA Ops:
  0.6 64.6 %exchange.1 = (f32[640,2048]{1,0:T(8,128)}, bf16[640,256]{1,0:T(8,128)(2,1)}, bf16[256,2048]{1,0:T(8,128)(2,1)}) custom-call(bf16[576,4096]{1,0:T(8,128)(2,1)} %e.1, bf16[320,2048]{1,0:T(8,128)(2,1)} %bitcast.7, bf16[320,2048]{1,0:T(8,128)(2,1)} %bitcast.8, s32[576]{0:T(1024)} %folds.1, s32[576]{0:T(1024)} %labels.1), custom_call_target="tpu_custom_call" | custom-call | tf_op jit(solution)/shard_map/exchange/pallas_call | solution.py:385
  65.3 6.2 %product.1 = (f32[320,2048]{1,0:T(8,128)}, f32[320,2048]{1,0:T(8,128)}) custom-call(f32[2,320,2048]{2,1,0:T(8,128)} %bitcast.6, bf16[2,320,256]{2,1,0:T(8,128)(2,1)} %bitcast.9, bf16[256,2048]{1,0:T(8,128)(2,1)} %get-tuple-element.9.etail), custom_call_target="tpu_custom_call" | custom-call | tf_op jit(solution)/shard_map/product/pallas_call | solution.py:425
